TPU v7x, 32 devices: a whole 2x2x4 slice. The times are simulated.
32 devices in a mesh: row: 8 (over y, x, core), col: 4 (over z).
Axes of the slice: x: 2, y: 2, z: 4, core: 2. Of those that a mesh axis runs over, the one named last changes fastest.
Arguments:
- screen: int32 [1536, 3], P(('row', 'col')), may hold values from 0 to 31, as said below
- values: bfloat16 [1536, 128, 128], P(('row', 'col')), may hold values from -6 to 6
- sizes: int32 [32], replicated, may hold values from 64 to 128
- slot: int32 [32], replicated, may hold values from 0 to 31, as said below
- orbitals: bfloat16 [4096, 512], P('col'), may hold values from -0.15625 to 0.15625
Outputs:
- half_transformed: bfloat16 [4096, 4, 512], P(('row', 'col'))
Inputs may be any that keep to these rules, and one draw needn't show every extreme that they name: `screen`: columns hold a, b, q with a and b below 32 and q below 4. The rows of device d (rows d * 48 onward, devices in row-major order) name blocks b in column group d % 4, that is b // 8 equals it. Among one device's rows at most 6 have slot[a] // 4 equal to any one value, and on every device some value is taken by exactly 6 rows. Triples may repeat. `slot`: A permutation of the block numbers.
All inputs are finite; a program needn't handle non-finite values.
Results may differ from a plain program's by a relative error of at most 0.0015.
Values may be sent and summed in bfloat16 or wider, within the bound.
A program may use at most 64 MiB of HBM per device.

v0:
```python
import math

import jax
import jax.numpy as jnp
from jax import lax
from jax.sharding import PartitionSpec as P

NQ = 4


def on_device(screen, values, sizes, slot, orbitals):
    row_count = lax.axis_size("row")
    col_count = lax.axis_size("col")
    blocks_all = sizes.shape[0]
    width = values.shape[1]
    orbital_count = orbitals.shape[1]
    per_row = blocks_all // row_count
    per_col = blocks_all // col_count
    listed = screen.shape[0]
    capacity = max(4, -(-listed // row_count))
    slots_all = row_count * capacity
    placed = slot[screen[:, 0]]
    owner = placed // per_row
    hits = (owner[:, None] == jnp.arange(row_count, dtype=jnp.int32)[None, :]).astype(jnp.int32)
    rank_in = jnp.sum(jnp.cumsum(hits, axis=0) * hits, axis=1) - 1
    position = owner * capacity + rank_in
    labels = jnp.stack([placed % per_row, screen[:, 1] % per_col, screen[:, 2]], axis=1)
    send_values = jnp.zeros((slots_all, width, width), values.dtype).at[position].set(values)
    send_labels = jnp.zeros((slots_all, 3), jnp.int32).at[position].set(labels)
    got_values, got_labels = (
        lax.all_to_all(
            send_values.reshape(row_count, capacity, width, width),
            "row",
            split_axis=0,
            concat_axis=0,
            tiled=True,
        ),
        lax.all_to_all(
            send_labels.reshape(row_count, capacity, 3),
            "row",
            split_axis=0,
            concat_axis=0,
            tiled=True,
        ),
    )
    got_values = got_values.reshape(slots_all, width, width)
    got_labels = got_labels.reshape(slots_all, 3)
    col_index = lax.axis_index("col")
    local_sizes = lax.dynamic_slice_in_dim(sizes, col_index * per_col, per_col)
    keep = (jnp.arange(width)[None, :] < local_sizes[:, None]).astype(orbitals.dtype)
    coeffs = orbitals.reshape(per_col, width, orbital_count) * keep[:, :, None]
    a_range = jnp.arange(per_row, dtype=jnp.int32)
    q_range = jnp.arange(NQ, dtype=jnp.int32)
    group = math.gcd(slots_all, 16)
    rounds = slots_all // group

    def accumulate(running, batch):
        block_vals, block_labels = batch
        picked = coeffs[block_labels[:, 1]]
        product = jnp.einsum("gmn,gno->gmo", block_vals, picked, preferred_element_type=jnp.float32)
        pick_a = (block_labels[:, 0:1] == a_range[None, :]).astype(jnp.float32)
        pick_q = (block_labels[:, 2:3] == q_range[None, :]).astype(jnp.float32)
        running = running + jnp.einsum(
            "ga,gq,gmo->amqo", pick_a, pick_q, product, precision=lax.Precision.HIGHEST
        )
        return (running, None)

    start = jnp.zeros((per_row, width, NQ, orbital_count), jnp.float32)
    totals, unused = lax.scan(
        accumulate,
        start,
        (got_values.reshape(rounds, group, width, width), got_labels.reshape(rounds, group, 3)),
    )
    term = totals.reshape(per_row * width, NQ, orbital_count)
    summed = lax.psum_scatter(term, "col", scatter_dimension=0, tiled=True)
    rows_out = summed.shape[0]
    row_index = lax.axis_index("row")
    first_row = (row_index * col_count + col_index) * rows_out
    global_rows = first_row + jnp.arange(rows_out, dtype=jnp.int32)
    inverse = (
        jnp.zeros((blocks_all,), jnp.int32).at[slot].set(jnp.arange(blocks_all, dtype=jnp.int32))
    )
    slot_sizes = sizes[inverse]
    live = (global_rows % width < slot_sizes[global_rows // width]).astype(jnp.float32)
    return (summed * live[:, None, None]).astype(jnp.bfloat16)


def solution(mesh):
    in_specs = (P(("row", "col"), None), P(("row", "col"), None, None), P(), P(), P("col", None))
    out_specs = P(("row", "col"), None, None)
    return jax.shard_map(
        on_device, mesh=mesh, in_specs=in_specs, out_specs=out_specs, check_vma=False
    )
```

profile of v0, /device:TPU:9, one launch (start us, length us, event | category | flops | bytes accessed | tf_op | source)
XLA Modules:
  0.0 260.7 jit_solution(8273956968907952758)
XLA Ops:
  6.5 0.8 and_select_fusion.2
  7.3 1.4 gather_fusion.1
  9.3 0.7 scatter_custom_fusion
  10.1 0.6 copy.14
  10.8 4.4 %all-to-all-start = ((s32[8,6,3]{1,2,0:T(4,128)}), s32[8,6,3]{1,2,0:T(4,128)S(1)}, u32[]{:S(2)}, u32[]{:S(2)}) async-start(s32[8,6,3]{1,2,0:T(4,128)} %copy.14), calls=%async_computation | async-start | bytes 32768 | tf_op jit(solution)/shard_map/all_to_all | solution.py:38
  15.1 1.6 broadcast_in_dim.18
  16.7 7.6 %scatter_fusion = bf16[48,128,128]{2,1,0:T(8,128)(2,1)} fusion(bf16[48,128,128]{2,1,0:T(8,128)(2,1)} %broadcast_in_dim.18, s32[48]{0:T(128)S(1)} %get-tuple-element.124, bf16[48,128,128]{2,1,0:T(8,128)(2,1)} %param.8), kind=kCustom, calls=%fused_computation.5 | custom fusion | bytes 4718784 | tf_op jit(solution)/shard_map/scatter | solution.py:28
  24.4 4.3 %all-to-all-start.1 = ((bf16[8,6,128,128]{3,2,1,0:T(8,128)(2,1)}), bf16[8,6,128,128]{3,2,1,0:T(8,128)(2,1)S(1)}, u32[]{:S(2)}, u32[]{:S(2)}) async-start(bf16[8,6,128,128]{3,2,1,0:T(8,128)(2,1)} %bitcast.4), calls=%async_computation.1 | async-start | bytes 3145728 | tf_op jit(solution)/shard_map/all_to_all | solution.py:31
  28.8 1.4 broadcast_multiply_fusion
  30.3 15.9 %all-to-all-done.1 = bf16[8,6,128,128]{3,2,1,0:T(8,128)(2,1)S(1)} async-done(((bf16[8,6,128,128]{3,2,1,0:T(8,128)(2,1)}), bf16[8,6,128,128]{3,2,1,0:T(8,128)(2,1)S(1)}, u32[]{:S(2)}, u32[]{:S(2)}) %all-to-all-start.1) | async-done | bytes 1572896 | tf_op jit(solution)/shard_map/all_to_all | solution.py:31
  46.2 43.2 %while.13 = (s32[]{:T(128)}, f32[4,128,4,512]{3,0,1,2:T(4,128)}, s32[3,16,3]{1,0,2:T(4,128)S(1)}, bf16[3,16,128,128]{3,2,1,0:T(8,128)(2,1)S(1)}, bf16[8,128,512]{2,1,0:T(8,128)(2,1)S(1)}, /*index=5*/s32[]{:T(128)}, s32[]{:T(128)}) while((s32[]{:T(128)}, f32[4,128,4,512]{3,0,1,2:T(4,128)}, s32[3,16,3]{1,0,2:T(4,128)S(1)}, ...), condition=%wide.region_5.6_spmd.clone.clone, body=%wide.region_4.5_spmd.clone.clone.sunk | while | flops 471860800 | bytes 69737048 | solution.py:69
  46.2 1.1 copy-done.4
  47.4 0.7 gather_fusion
  48.1 1.9 fusion.41
  50.4 8.2 %bitcast_add_fusion.3 = f32[4,128,4,512]{3,0,1,2:T(4,128)S(1)} fusion(f32[4,128,4,512]{3,0,1,2:T(4,128)S(1)} %copy-done.2, f32[16,128,512]{2,1,0:T(8,128)S(1)} %fusion.41, pred[]{:T(512)S(6)} %compare.37, f32[16,4]{0,1:T(4,128)S(1)} %get-tuple-element.164, f32[16,4]{0,1:T(4,128)S(1)} %get-tuple-element.165), kind=kOutput, calls=%fused_computation.8.clone.1 | convolution fusion | flops 203424000 | bytes 12583425 | tf_op jit(solution)/shard_map/while/body/eval_jaxpr/ga,gq,gmo->amqo/dot_general | solution.py:63
  58.7 1.9 copy-done.3
  60.7 1.1 copy-done.4
  61.8 0.7 gather_fusion
  62.5 1.9 fusion.41
  64.8 8.2 %bitcast_add_fusion.3 = f32[4,128,4,512]{3,0,1,2:T(4,128)S(1)} fusion(f32[4,128,4,512]{3,0,1,2:T(4,128)S(1)} %copy-done.2, f32[16,128,512]{2,1,0:T(8,128)S(1)} %fusion.41, pred[]{:T(512)S(6)} %compare.37, f32[16,4]{0,1:T(4,128)S(1)} %get-tuple-element.164, f32[16,4]{0,1:T(4,128)S(1)} %get-tuple-element.165), kind=kOutput, calls=%fused_computation.8.clone.1 | convolution fusion | flops 203424000 | bytes 12583425 | tf_op jit(solution)/shard_map/while/body/eval_jaxpr/ga,gq,gmo->amqo/dot_general | solution.py:63
  73.1 1.9 copy-done.3
  75.1 1.1 copy-done.4
  76.2 0.7 gather_fusion
  76.9 1.9 fusion.41
  79.2 8.2 %bitcast_add_fusion.3 = f32[4,128,4,512]{3,0,1,2:T(4,128)S(1)} fusion(f32[4,128,4,512]{3,0,1,2:T(4,128)S(1)} %copy-done.2, f32[16,128,512]{2,1,0:T(8,128)S(1)} %fusion.41, pred[]{:T(512)S(6)} %compare.37, f32[16,4]{0,1:T(4,128)S(1)} %get-tuple-element.164, f32[16,4]{0,1:T(4,128)S(1)} %get-tuple-element.165), kind=kOutput, calls=%fused_computation.8.clone.1 | convolution fusion | flops 203424000 | bytes 12583425 | tf_op jit(solution)/shard_map/while/body/eval_jaxpr/ga,gq,gmo->amqo/dot_general | solution.py:63
  87.5 1.9 copy-done.3
  89.4 6.8 %copy.17 = f32[4,128,4,512]{3,2,1,0:T(4,128)} copy(f32[4,128,4,512]{3,0,1,2:T(4,128)} %get-tuple-element.58) | data formatting | bytes 8388608 | tf_op jit(solution)/shard_map/while | solution.py:69
  96.9 0.7 scatter_custom_fusion.2
  97.7 0.7 gather_fusion.2
  99.6 1.2 gather_fusion.3
  100.9 150.7 %all-reduce.3.cloned.1.call-done = f32[512,4,512]{2,1,0:T(4,128)} async-done(((f32[512,4,512]{2,1,0:T(4,128)}), f32[512,4,512]{2,1,0:T(4,128)}) %all-reduce.3.cloned.1.call-update) | async-done | bytes 4194320
  251.6 2.3 fusion.18
  (65 shorter events, 3.6 us)
Async XLA Ops:
  10.8 13.6 %all-to-all-start = ((s32[8,6,3]{1,2,0:T(4,128)}), s32[8,6,3]{1,2,0:T(4,128)S(1)}, u32[]{:S(2)}, u32[]{:S(2)}) async-start(s32[8,6,3]{1,2,0:T(4,128)} %copy.14), calls=%async_computation | async-start | bytes 32768 | tf_op jit(solution)/shard_map/all_to_all | solution.py:38
  16.7 11.9 %copy-start.1 = (s32[32]{0:T(128)S(1)}, s32[32]{0:T(128)}, u32[]{:S(2)}) copy-start(s32[32]{0:T(128)} %param.9) | copy-start | bytes 388
  24.4 21.8 %all-to-all-start.1 = ((bf16[8,6,128,128]{3,2,1,0:T(8,128)(2,1)}), bf16[8,6,128,128]{3,2,1,0:T(8,128)(2,1)S(1)}, u32[]{:S(2)}, u32[]{:S(2)}) async-start(bf16[8,6,128,128]{3,2,1,0:T(8,128)(2,1)} %bitcast.4), calls=%async_computation.1 | async-start | bytes 3145728 | tf_op jit(solution)/shard_map/all_to_all | solution.py:31
  28.6 223.0 %all-reduce.3.cloned.1.call-start = ((), (), s32[]{:S(2)}) async-start(), calls=%async_computation.2 | async-start | bytes 8388608
  46.2 1.2 copy-start.4
  48.1 2.3 copy-start.2
  50.4 10.2 %copy-start.5 = (bf16[3,16,128,128]{3,2,1,0:T(8,128)(2,1)S(1)}, bf16[3,16,128,128]{3,2,1,0:T(8,128)(2,1)}, u32[]{:S(2)}) copy-start(bf16[3,16,128,128]{3,2,1,0:T(8,128)(2,1)} %copy-done.4) | copy-start | bytes 4718596 | tf_op jit(solution)/shard_map/while
  58.7 1.9 copy-start.3
  60.6 1.2 copy-start.4
  62.5 2.3 copy-start.2
  64.8 10.2 %copy-start.5 = (bf16[3,16,128,128]{3,2,1,0:T(8,128)(2,1)S(1)}, bf16[3,16,128,128]{3,2,1,0:T(8,128)(2,1)}, u32[]{:S(2)}) copy-start(bf16[3,16,128,128]{3,2,1,0:T(8,128)(2,1)} %copy-done.4) | copy-start | bytes 4718596 | tf_op jit(solution)/shard_map/while
  73.1 1.9 copy-start.3
  75.0 1.2 copy-start.4
  76.9 2.3 copy-start.2
  79.2 10.2 %copy-start.5 = (bf16[3,16,128,128]{3,2,1,0:T(8,128)(2,1)S(1)}, bf16[3,16,128,128]{3,2,1,0:T(8,128)(2,1)}, u32[]{:S(2)}) copy-start(bf16[3,16,128,128]{3,2,1,0:T(8,128)(2,1)} %copy-done.4) | copy-start | bytes 4718596 | tf_op jit(solution)/shard_map/while
  87.5 1.9 copy-start.3
  96.3 0.7 copy-start
  96.3 2.1 copy-start.6
Sparse Core Ops, SparseCore 0:
  96.4 155.1 all-reduce.2
where the time goes:
time: 265 us; the launch traced here: 261 us
  waiting for transfers between devices  167 us (63%)
  local copies, waits for them, and re-layouts  35.6 us (13%)
  matrix products  30.4 us (11%)
  between operations  14.2 us (5%)
  starting transfers between devices  8.65 us (3%)
  other arithmetic  5.05 us (2%)
    unnamed x2, waiting for transfers between devices  151 us
    dot_general x3, matrix products, accumulate(): jnp.einsum('ga,gq,gmo->amqo', pick_a, pick_q, product, precision=lax.Prec...  24.7 us
    all_to_all x1, waiting for transfers between devices, on_device(): lax.all_to_all(send_values.reshape(row_count, capacity, width, width), 'r...  15.9 us
    while x24, local copies, waits for them, and re-layouts  10.5 us
    scatter x1, local copies, waits for them, and re-layouts, on_device(): jnp.zeros((slots_all, width, width), values.dtype).at[position].set(values)  7.65 us
    while x1, local copies, waits for them, and re-layouts, on_device(): lax.scan(accumulate, start, (got_values.reshape(rounds, group, width, wid...  6.85 us
    dot_general x3, matrix products, accumulate(): jnp.einsum('gmn,gno->gmo', block_vals, picked, preferred_element_type=jnp...  5.68 us
  transfers between devices with their start and end apart: 3, of which 2 were waited for; matrix products, arithmetic and copies ran while one was open for 5% of the time, Pallas kernels for 0%

commit v1 on v0

v1 whole, which is shorter than its diff:
```python
import functools

import jax
import jax.numpy as jnp
from jax import lax
from jax.experimental import pallas as pl
from jax.experimental.pallas import tpu as pltpu
from jax.sharding import PartitionSpec as P

NQ = 4
LANES = 128
VMEM_LIMIT = 48 * 1024 * 1024


def order_kernel(rows, capacity, per_row, per_col, screen_ref, slot_ref, order_ref, label_ref, count):
    listed = screen_ref.shape[0]

    @pl.loop(0, rows)
    def clear(r):
        count[r] = 0

    @pl.loop(0, rows * capacity)
    def empty(k):
        order_ref[k] = 0
        label_ref[k] = -1

    @pl.loop(0, listed)
    def place(k):
        placed = slot_ref[screen_ref[k, 0]]
        owner = placed // per_row
        seat = owner * capacity + count[owner]
        count[owner] = count[owner] + 1
        order_ref[seat] = k
        out_block = (placed % per_row) * NQ + screen_ref[k, 2]
        label_ref[seat] = out_block * per_col + screen_ref[k, 1] % per_col


def exchange_kernel(
    rows, capacity, order_ref, label_ref, values_ref, got_ref, got_label_ref,
    send, send_label, send_sem, recv_sem, send_label_sem, recv_label_sem,
):
    me = lax.axis_index("row")
    barrier = pltpu.get_barrier_semaphore()
    for step in range(1, rows):
        pl.semaphore_signal(
            barrier, inc=1, device_id={"row": lax.rem(me + step, rows)},
            device_id_type=pl.DeviceIdType.MESH,
        )
    lane = lax.broadcasted_iota(jnp.int32, (1, LANES), 1)

    def fill_label(row):
        line = jnp.full((1, LANES), -1, jnp.int32)
        for j in range(capacity):
            line = jnp.where(lane == j, label_ref[row * capacity + j], line)
        return line

    def copies(step):
        target = lax.rem(me + step, rows)
        return (
            pltpu.make_async_remote_copy(
                src_ref=send.at[step - 1],
                dst_ref=got_ref.at[pl.ds(step * capacity, capacity)],
                send_sem=send_sem.at[step - 1],
                recv_sem=recv_sem.at[step - 1],
                device_id={"row": target},
                device_id_type=pl.DeviceIdType.MESH,
            ),
            pltpu.make_async_remote_copy(
                src_ref=send_label.at[step - 1],
                dst_ref=got_label_ref.at[step],
                send_sem=send_label_sem.at[step - 1],
                recv_sem=recv_label_sem.at[step - 1],
                device_id={"row": target},
                device_id_type=pl.DeviceIdType.MESH,
            ),
        )

    pl.semaphore_wait(barrier, rows - 1)
    for step in range(1, rows):
        target = lax.rem(me + step, rows)
        for j in range(capacity):
            send[step - 1, j] = values_ref[order_ref[target * capacity + j]]
        send_label[step - 1] = fill_label(target)
        for copy in copies(step):
            copy.start()
    for j in range(capacity):
        got_ref[j] = values_ref[order_ref[me * capacity + j]]
    got_label_ref[0] = fill_label(me)
    for step in range(1, rows):
        for copy in copies(step):
            copy.wait()


def contract_kernel(
    capacity, per_col, label_ref, sizes_ref, got_ref, orbitals_ref,
    packed_ref, unit_ref, own_ref, totals, coeffs,
):
    width = got_ref.shape[1]
    cols, nq, rows_out, _ = packed_ref.shape
    splits = width // rows_out
    col = lax.axis_index("col")
    vertical = lax.broadcasted_iota(jnp.int32, (width, 1), 0)
    for b in range(per_col):
        size = sizes_ref[col * per_col + b]
        block = orbitals_ref[pl.ds(b * width, width), :].astype(jnp.float32)
        coeffs[b] = jnp.where(vertical < size, block, 0.0).astype(coeffs.dtype)

    @pl.loop(0, totals.shape[0])
    def clear(t):
        totals[t] = jnp.zeros(totals.shape[1:], jnp.float32)

    @pl.loop(0, got_ref.shape[0])
    def add(k):
        label = label_ref[k // capacity, 0, k % capacity]

        @pl.when(label >= 0)
        def listed():
            totals[label // per_col] += jnp.dot(
                got_ref[k], coeffs[label % per_col], preferred_element_type=jnp.float32
            )

    def tile(c, q):
        return totals[
            (c // splits) * nq + q, pl.ds(pl.multiple_of((c % splits) * rows_out, rows_out), rows_out)
        ]

    @pl.loop(0, cols * nq)
    def code(t):
        c, q = t // nq, t % nq
        part = tile(c, q)
        top = jnp.max(jnp.max(jnp.abs(part), axis=0, keepdims=True), axis=1, keepdims=True)
        unit = jnp.maximum(top, 1e-30) * 2.0**-15
        unit_ref[c, q] = jnp.broadcast_to(unit, (8, LANES))
        scaled = part * (1.0 / unit)
        power = scaled * scaled
        power = power * power
        power = power * power
        packed_ref[c, q] = jnp.where(scaled < 0.0, -power, power).astype(packed_ref.dtype)

    for q in range(nq):
        own_ref[q] = tile(col, q)


def scatter_kernel(
    cols, blocks_all, width, slot_ref, sizes_ref, packed_ref, unit_ref, own_ref, out_ref,
    got, got_unit, total, send_sem, recv_sem, send_unit_sem, recv_unit_sem,
):
    me = lax.axis_index("col")
    nq, rows_out, _ = own_ref.shape
    barrier = pltpu.get_barrier_semaphore()
    for step in range(1, cols):
        pl.semaphore_signal(
            barrier, inc=1, device_id={"col": lax.rem(me + step, cols)},
            device_id_type=pl.DeviceIdType.MESH,
        )
    pl.semaphore_wait(barrier, cols - 1)

    def unit_copy(step):
        target = lax.rem(me + step, cols)
        return pltpu.make_async_remote_copy(
            src_ref=unit_ref.at[target],
            dst_ref=got_unit.at[step - 1],
            send_sem=send_unit_sem.at[step - 1],
            recv_sem=recv_unit_sem.at[step - 1],
            device_id={"col": target},
            device_id_type=pl.DeviceIdType.MESH,
        )

    def part_copy(step, q):
        target = lax.rem(me + step, cols)
        return pltpu.make_async_remote_copy(
            src_ref=packed_ref.at[target, q],
            dst_ref=got.at[step - 1, q],
            send_sem=send_sem.at[step - 1, q],
            recv_sem=recv_sem.at[step - 1, q],
            device_id={"col": target},
            device_id_type=pl.DeviceIdType.MESH,
        )

    for step in range(1, cols):
        unit_copy(step).start()
    for q in range(nq):
        for step in range(1, cols):
            part_copy(step, q).start()

    first_row = (lax.axis_index("row") * cols + me) * rows_out
    mine = first_row // width
    size = jnp.int32(0)
    for b in range(blocks_all):
        size = jnp.where(slot_ref[b] == mine, sizes_ref[b], size)
    vertical = lax.broadcasted_iota(jnp.int32, (rows_out, 1), 0) + lax.rem(first_row, width)
    live = vertical < size

    for step in range(1, cols):
        unit_copy(step).wait()
    for q in range(nq):
        for step in range(1, cols):
            part_copy(step, q).wait()
            coded = got[step - 1, q].astype(jnp.float32)
            root = jnp.exp(0.125 * jnp.log(jnp.abs(coded)))
            root = jnp.where(coded < 0.0, -root, jnp.where(coded > 0.0, root, 0.0))
            before = own_ref[q] if step == 1 else total[...]
            total[...] = before + root * got_unit[step - 1, q, 0:1, 0:1]
        out_ref[q] = jnp.where(live, total[...], 0.0).astype(out_ref.dtype)


def on_device(screen, values, sizes, slot, orbitals):
    rows = lax.axis_size("row")
    cols = lax.axis_size("col")
    blocks_all = sizes.shape[0]
    listed, width = values.shape[:2]
    orbital_count = orbitals.shape[1]
    per_row = blocks_all // rows
    per_col = blocks_all // cols
    capacity = max(4, -(-listed // rows))
    seats = rows * capacity
    smem = pl.BlockSpec(memory_space=pltpu.SMEM)
    vmem = pl.BlockSpec(memory_space=pltpu.VMEM)
    dma = pltpu.SemaphoreType.DMA

    order, labels = pl.pallas_call(
        functools.partial(order_kernel, rows, capacity, per_row, per_col),
        out_shape=[jax.ShapeDtypeStruct((seats,), jnp.int32)] * 2,
        in_specs=[smem] * 2,
        out_specs=[smem] * 2,
        scratch_shapes=[pltpu.SMEM((rows,), jnp.int32)],
        name="order_blocks",
    )(screen, slot)

    got, got_labels = pl.pallas_call(
        functools.partial(exchange_kernel, rows, capacity),
        out_shape=[
            jax.ShapeDtypeStruct((seats, width, width), values.dtype),
            jax.ShapeDtypeStruct((rows, 1, LANES), jnp.int32),
        ],
        in_specs=[smem, smem, vmem],
        out_specs=[vmem] * 2,
        scratch_shapes=[
            pltpu.VMEM((rows - 1, capacity, width, width), values.dtype),
            pltpu.VMEM((rows - 1, 1, LANES), jnp.int32),
            dma((rows - 1,)), dma((rows - 1,)), dma((rows - 1,)), dma((rows - 1,)),
        ],
        compiler_params=pltpu.CompilerParams(
            collective_id=0, has_side_effects=True, vmem_limit_bytes=VMEM_LIMIT
        ),
        name="exchange_blocks",
    )(order, labels, values)

    rows_out = per_row * width // cols
    packed, units, own = pl.pallas_call(
        functools.partial(contract_kernel, capacity, per_col),
        out_shape=[
            jax.ShapeDtypeStruct((cols, NQ, rows_out, orbital_count), jnp.bfloat16),
            jax.ShapeDtypeStruct((cols, NQ, 8, LANES), jnp.float32),
            jax.ShapeDtypeStruct((NQ, rows_out, orbital_count), jnp.float32),
        ],
        in_specs=[smem, smem, vmem, vmem],
        out_specs=[vmem] * 3,
        scratch_shapes=[
            pltpu.VMEM((per_row * NQ, width, orbital_count), jnp.float32),
            pltpu.VMEM((per_col, width, orbital_count), orbitals.dtype),
        ],
        compiler_params=pltpu.CompilerParams(vmem_limit_bytes=VMEM_LIMIT),
        name="contract_blocks",
    )(got_labels, sizes, got, orbitals)

    summed = pl.pallas_call(
        functools.partial(scatter_kernel, cols, blocks_all, width),
        out_shape=jax.ShapeDtypeStruct((NQ, rows_out, orbital_count), jnp.bfloat16),
        in_specs=[smem, smem, vmem, vmem, vmem],
        out_specs=vmem,
        scratch_shapes=[
            pltpu.VMEM((cols - 1, NQ, rows_out, orbital_count), jnp.bfloat16),
            pltpu.VMEM((cols - 1, NQ, 8, LANES), jnp.float32),
            pltpu.VMEM((rows_out, orbital_count), jnp.float32),
            dma((cols - 1, NQ)), dma((cols - 1, NQ)), dma((cols - 1,)), dma((cols - 1,)),
        ],
        compiler_params=pltpu.CompilerParams(
            collective_id=1, has_side_effects=True, vmem_limit_bytes=VMEM_LIMIT
        ),
        name="scatter_sums",
    )(slot, sizes, packed, units, own)
    return summed.transpose(1, 0, 2)


def solution(mesh):
    in_specs = (P(("row", "col"), None), P(("row", "col"), None, None), P(), P(), P("col", None))
    out_specs = P(("row", "col"), None, None)
    return jax.shard_map(
        on_device, mesh=mesh, in_specs=in_specs, out_specs=out_specs, check_vma=False
    )
```

time: 265 us -> 95.5 us (0.36); the launches traced: 261 us -> 95.2 us
  waiting for transfers between devices: 167 us -> 0 us
  Pallas kernels: 0 us -> 89.8 us
  matrix products: 30.4 us -> 0 us
  local copies, waits for them, and re-layouts: 35.6 us -> 5.32 us
  between operations: 14.2 us -> 0.08 us
  starting transfers between devices: 8.65 us -> 0 us
  other arithmetic: 5.05 us -> 0 us
    unnamed x2 -> x0, waiting for transfers between devices: 151 us -> none
    pallas_call x0 -> x4, Pallas kernels: none -> 89.8 us  [the longest x1 51 us: on_device(): pl.pallas_call(functools.partial(scatter_kernel, cols, blocks_all, width)...]
    dot_general x6 -> x0, matrix products: 30.4 us -> none  [the longest x3 24.7 us: accumulate(): jnp.einsum('ga,gq,gmo->amqo', pick_a, pick_q, product, precision=lax.Prec...]
    while x25 -> x0, local copies, waits for them, and re-layouts: 17.4 us -> none
    all_to_all x2 -> x0, waiting for transfers between devices: 15.9 us -> none  [the longest x1 15.9 us: on_device(): lax.all_to_all(send_values.reshape(row_count, capacity, width, width), 'r...]
    scatter x4 -> x0, local copies, waits for them, and re-layouts: 9.1 us -> none  [the longest x1 7.65 us: on_device(): jnp.zeros((slots_all, width, width), values.dtype).at[position].set(values)]
    all_to_all x2 -> x0, starting transfers between devices: 8.65 us -> none  [the longest x1 4.39 us: on_device(): lax.all_to_all(send_labels.reshape(row_count, capacity, 3), 'row', split_...]
    gather x6 -> x0, local copies, waits for them, and re-layouts: 5.39 us -> none  [the longest x3 2.04 us: accumulate(): picked = coeffs[block_labels[:, 1]]]
  transfers between devices with their start and end apart: 3 -> 0, of which waited for: 2 -> 0; matrix products, arithmetic and copies ran while one was open for 5% -> 0% of each run, Pallas kernels for 0% -> 0%
where the time goes in v1:
time: 95.5 us; the launch traced here: 95.2 us
  Pallas kernels  89.8 us (94%)
  local copies, waits for them, and re-layouts  5.32 us (6%)
    pallas_call x1, Pallas kernels, on_device(): pl.pallas_call(functools.partial(scatter_kernel, cols, blocks_all, width)...  51 us
    pallas_call x1, Pallas kernels, on_device(): pl.pallas_call(functools.partial(exchange_kernel, rows, capacity), out_sh...  21.9 us
    pallas_call x1, Pallas kernels, on_device(): pl.pallas_call(functools.partial(contract_kernel, capacity, per_col), out...  13.8 us
    unnamed x13, local copies, waits for them, and re-layouts  4.12 us
    pallas_call x1, Pallas kernels, on_device(): pl.pallas_call(functools.partial(order_kernel, rows, capacity, per_row, p...  3.1 us

profile of v1, /device:TPU:9, one launch (start us, length us, event | category | flops | bytes accessed | tf_op | source)
XLA Modules:
  0.0 95.2 jit_solution(3587221478128013060)
XLA Ops:
  0.0 0.0 copy-start.3
  0.0 1.4 %copy.6.screen_ref = s32[48,3]{1,0:T(8,128)} copy(s32[48,3]{0,1:T(4,128)} %param.5) | data formatting | bytes 1152 | tf_op args[0]
  1.4 3.1 %order_blocks.1 = (s32[48]{0:T(128)}, s32[48]{0:T(128)}) custom-call(s32[48,3]{1,0:T(8,128)} %copy.6.screen_ref, s32[32]{0:T(128)} %slot_ref.3), custom_call_target="tpu_custom_call" | custom-call | tf_op jit(solution)/shard_map/order_blocks/pallas_call | solution.py:221
  4.5 0.0 copy-start
  4.5 1.4 %copy-done = bf16[48,128,128]{2,1,0:T(8,128)(2,1)S(1)} copy-done((bf16[48,128,128]{2,1,0:T(8,128)(2,1)S(1)}, bf16[48,128,128]{2,1,0:T(8,128)(2,1)}, u32[]{:S(2)}) %copy-start) | copy-done | bytes 1572888
  5.9 0.0 copy-start.4
  5.9 0.7 copy-done.4
  6.6 0.0 copy-start.5
  6.6 0.7 copy-done.5
  7.2 0.0 copy-start.1
  7.2 21.9 %exchange_blocks.1 = (bf16[48,128,128]{2,1,0:T(8,128)(2,1)S(1)}, s32[8,1,128]{2,1,0:T(1,128)S(1)}) custom-call(s32[48]{0:T(128)S(1)} %copy-done.4, s32[48]{0:T(128)S(1)} %copy-done.5, bf16[48,128,128]{2,1,0:T(8,128)(2,1)S(1)} %copy-done), custom_call_target="tpu_custom_call" | custom-call | tf_op jit(solution)/shard_map/exchange_blocks/pallas_call | solution.py:230
  29.1 0.0 copy-start.2
  29.1 0.0 copy-done.3
  29.1 0.0 copy-done.1
  29.1 13.8 %contract_blocks.1 = (bf16[4,4,128,512]{3,2,1,0:T(8,128)(2,1)S(1)}, f32[4,4,8,128]{3,2,1,0:T(8,128)S(1)}, f32[4,128,512]{2,1,0:T(8,128)S(1)}) custom-call(s32[8,1,128]{2,1,0:T(1,128)S(1)} %get-tuple-element.14.label_ref, s32[32]{0:T(128)S(1)} %copy-done.3, bf16[48,128,128]{2,1,0:T(8,128)(2,1)S(1)} %get-tuple-element.15.got_ref, bf16[1024,512]{1,0:T(8,128)(2,1)S(1)} %copy-done.1), custom_call_target="tpu_custom_call" | custom-call | tf_op jit(solution)/shard_map/contract_blocks/pallas_call | solution.py:250
  43.0 0.0 copy-done.2
  43.0 51.0 %scatter_sums.1 = bf16[4,128,512]{2,1,0:T(8,128)(2,1)S(1)} custom-call(s32[32]{0:T(128)S(1)} %copy-done.2, s32[32]{0:T(128)S(1)} %copy-done.3, bf16[4,4,128,512]{3,2,1,0:T(8,128)(2,1)S(1)} %get-tuple-element.16.packed_ref, f32[4,4,8,128]{3,2,1,0:T(8,128)S(1)} %get-tuple-element.17.unit_ref, f32[4,128,512]{2,1,0:T(8,128)S(1)} %get-tuple-element.18.own_ref), custom_call_target="tpu_custom_call" | custom-call | tf_op jit(solution)/shard_map/scatter_sums/pallas_call | solution.py:267
  94.0 1.2 %copy.7 = bf16[128,4,512]{2,1,0:T(4,128)(2,1)} copy(bf16[128,4,512]{2,0,1:T(8,128)(2,1)S(1)} %bitcast.1) | data formatting | bytes 1048576 | tf_op jit(solution)/shard_map/transpose | solution.py:283
Async XLA Ops:
  0.0 29.1 %copy-start.3 = (s32[32]{0:T(128)S(1)}, s32[32]{0:T(128)}, u32[]{:S(2)}) copy-start(s32[32]{0:T(128)} %sizes_ref.3) | copy-start | bytes 388
  4.5 1.4 %copy-start = (bf16[48,128,128]{2,1,0:T(8,128)(2,1)S(1)}, bf16[48,128,128]{2,1,0:T(8,128)(2,1)}, u32[]{:S(2)}) copy-start(bf16[48,128,128]{2,1,0:T(8,128)(2,1)} %values_ref.1) | copy-start | bytes 4718596
  5.9 0.7 copy-start.4
  6.6 0.7 copy-start.5
  7.2 21.9 %copy-start.1 = (bf16[1024,512]{1,0:T(8,128)(2,1)S(1)}, bf16[1024,512]{1,0:T(8,128)(2,1)}, u32[]{:S(2)}) copy-start(bf16[1024,512]{1,0:T(8,128)(2,1)} %orbitals_ref.1) | copy-start | bytes 3145732
  29.1 13.9 %copy-start.2 = (s32[32]{0:T(128)S(1)}, s32[32]{0:T(128)}, u32[]{:S(2)}) copy-start(s32[32]{0:T(128)} %slot_ref.3) | copy-start | bytes 388

commit v2 on v1

--- a/solution.py
+++ b/solution.py
@@ -9,7 +9,8 @@
 
 NQ = 4
 LANES = 128
-VMEM_LIMIT = 48 * 1024 * 1024
+LAG = 2
+VMEM_LIMIT = 20 * 1024 * 1024
 
 
 def order_kernel(rows, capacity, per_row, per_col, screen_ref, slot_ref, order_ref, label_ref, count):
@@ -19,12 +20,12 @@
     def clear(r):
         count[r] = 0
 
-    @pl.loop(0, rows * capacity)
+    @pl.loop(0, rows * capacity, unroll=8)
     def empty(k):
         order_ref[k] = 0
         label_ref[k] = -1
 
-    @pl.loop(0, listed)
+    @pl.loop(0, listed, unroll=8)
     def place(k):
         placed = slot_ref[screen_ref[k, 0]]
         owner = placed // per_row
@@ -92,12 +93,9 @@
 
 
 def contract_kernel(
-    capacity, per_col, label_ref, sizes_ref, got_ref, orbitals_ref,
-    packed_ref, unit_ref, own_ref, totals, coeffs,
+    capacity, per_col, label_ref, sizes_ref, got_ref, orbitals_ref, totals_ref, coeffs
 ):
     width = got_ref.shape[1]
-    cols, nq, rows_out, _ = packed_ref.shape
-    splits = width // rows_out
     col = lax.axis_index("col")
     vertical = lax.broadcasted_iota(jnp.int32, (width, 1), 0)
     for b in range(per_col):
@@ -105,48 +103,29 @@
         block = orbitals_ref[pl.ds(b * width, width), :].astype(jnp.float32)
         coeffs[b] = jnp.where(vertical < size, block, 0.0).astype(coeffs.dtype)
 
-    @pl.loop(0, totals.shape[0])
+    @pl.loop(0, totals_ref.shape[0])
     def clear(t):
-        totals[t] = jnp.zeros(totals.shape[1:], jnp.float32)
-
-    @pl.loop(0, got_ref.shape[0])
+        totals_ref[t] = jnp.zeros(totals_ref.shape[1:], jnp.float32)
+
+    @pl.loop(0, got_ref.shape[0], unroll=2)
     def add(k):
         label = label_ref[k // capacity, 0, k % capacity]
 
         @pl.when(label >= 0)
         def listed():
-            totals[label // per_col] += jnp.dot(
+            totals_ref[label // per_col] += jnp.dot(
                 got_ref[k], coeffs[label % per_col], preferred_element_type=jnp.float32
             )
 
-    def tile(c, q):
-        return totals[
-            (c // splits) * nq + q, pl.ds(pl.multiple_of((c % splits) * rows_out, rows_out), rows_out)
-        ]
-
-    @pl.loop(0, cols * nq)
-    def code(t):
-        c, q = t // nq, t % nq
-        part = tile(c, q)
-        top = jnp.max(jnp.max(jnp.abs(part), axis=0, keepdims=True), axis=1, keepdims=True)
-        unit = jnp.maximum(top, 1e-30) * 2.0**-15
-        unit_ref[c, q] = jnp.broadcast_to(unit, (8, LANES))
-        scaled = part * (1.0 / unit)
-        power = scaled * scaled
-        power = power * power
-        power = power * power
-        packed_ref[c, q] = jnp.where(scaled < 0.0, -power, power).astype(packed_ref.dtype)
-
-    for q in range(nq):
-        own_ref[q] = tile(col, q)
-
 
 def scatter_kernel(
-    cols, blocks_all, width, slot_ref, sizes_ref, packed_ref, unit_ref, own_ref, out_ref,
-    got, got_unit, total, send_sem, recv_sem, send_unit_sem, recv_unit_sem,
+    cols, blocks_all, slot_ref, sizes_ref, totals_ref, out_ref, send, got, total, send_sem, recv_sem
 ):
     me = lax.axis_index("col")
-    nq, rows_out, _ = own_ref.shape
+    nq, rows_out, orbital_count = out_ref.shape
+    width = totals_ref.shape[1]
+    splits = width // rows_out
+    sides = (me > 0, me < cols - 1)
     barrier = pltpu.get_barrier_semaphore()
     for step in range(1, cols):
         pl.semaphore_signal(
@@ -155,53 +134,104 @@
         )
     pl.semaphore_wait(barrier, cols - 1)
 
-    def unit_copy(step):
-        target = lax.rem(me + step, cols)
+    def copy(up, target, q):
         return pltpu.make_async_remote_copy(
-            src_ref=unit_ref.at[target],
-            dst_ref=got_unit.at[step - 1],
-            send_sem=send_unit_sem.at[step - 1],
-            recv_sem=recv_unit_sem.at[step - 1],
-            device_id={"col": target},
+            src_ref=send.at[target, q],
+            dst_ref=got.at[up, target, q],
+            send_sem=send_sem.at[target, q],
+            recv_sem=recv_sem.at[up, target, q],
+            device_id={"col": me + 1 if up else me - 1},
             device_id_type=pl.DeviceIdType.MESH,
         )
 
-    def part_copy(step, q):
-        target = lax.rem(me + step, cols)
-        return pltpu.make_async_remote_copy(
-            src_ref=packed_ref.at[target, q],
-            dst_ref=got.at[step - 1, q],
-            send_sem=send_sem.at[step - 1, q],
-            recv_sem=recv_sem.at[step - 1, q],
-            device_id={"col": target},
-            device_id_type=pl.DeviceIdType.MESH,
-        )
-
-    for step in range(1, cols):
-        unit_copy(step).start()
-    for q in range(nq):
-        for step in range(1, cols):
-            part_copy(step, q).start()
+    strip = min(rows_out, 32)
+
+    def own(c, q, at):
+        first = pl.multiple_of((c % splits) * rows_out + at, strip)
+        return totals_ref[(c // splits) * nq + q, pl.ds(first, strip)]
+
+    def decode(up, c, q, at, unit):
+        coded = got[up, c, q, pl.ds(at, strip), :].astype(jnp.float32)
+        root = jnp.exp2(0.125 * jnp.log2(jnp.abs(coded)))
+        return jnp.where(coded < 0.0, -root, root) * unit
+
+    def unit_of(up, c, q):
+        return got[up, c, q, pl.ds(rows_out, 16), :].astype(jnp.float32)[0:1, :]
+
+    def code(c, q, parts):
+        top = jnp.zeros((8, orbital_count), jnp.float32)
+        for at in range(0, rows_out, strip):
+            part = parts(at)
+            total[pl.ds(at, strip), :] = part
+            top = jnp.maximum(top, jnp.max(jnp.abs(part).reshape(-1, 8, orbital_count), axis=0))
+        top = jnp.max(jnp.max(top, axis=0, keepdims=True), axis=1, keepdims=True)
+        unit = (jnp.maximum(top, 1e-30) * (1.01 * 2.0**-15)).astype(send.dtype)
+        send[c, q, pl.ds(rows_out, 16), :] = jnp.broadcast_to(unit, (16, orbital_count))
+        inverse = 1.0 / unit.astype(jnp.float32)
+        for at in range(0, rows_out, strip):
+            scaled = total[pl.ds(at, strip), :] * inverse
+            power = scaled * scaled
+            power = power * power
+            power = power * power
+            send[c, q, pl.ds(at, strip), :] = jnp.where(scaled < 0.0, -power, power).astype(send.dtype)
+
+    @pl.loop(0, (cols - 1) * nq)
+    def ends(k):
+        i, q = k // nq, k % nq
+        for up, target, end in ((1, cols - 1 - i, 0), (0, i, cols - 1)):
+            @pl.when(me == end)
+            def begin():
+                code(target, q, lambda at: own(target, q, at))
+                copy(up, target, q).start()
+
+    tiles = (cols - 1) * nq
+
+    @pl.loop(0, tiles + (cols - 1) * LAG)
+    def between(k):
+        for up in (1, 0):
+            turn = k - LAG * (me if up else cols - 1 - me)
+            i, q = turn // nq, turn % nq
+            target = cols - 1 - i if up else i
+            inside = (me > 0) & (me < target) if up else (me < cols - 1) & (me > target)
+
+            @pl.when((turn >= 0) & (turn < tiles) & inside)
+            def forward():
+                copy(up, target, q).wait_recv()
+                unit = unit_of(up, target, q)
+                code(target, q, lambda at: own(target, q, at) + decode(up, target, q, at, unit))
+                copy(up, target, q).start()
 
     first_row = (lax.axis_index("row") * cols + me) * rows_out
     mine = first_row // width
     size = jnp.int32(0)
     for b in range(blocks_all):
         size = jnp.where(slot_ref[b] == mine, sizes_ref[b], size)
-    vertical = lax.broadcasted_iota(jnp.int32, (rows_out, 1), 0) + lax.rem(first_row, width)
-    live = vertical < size
-
-    for step in range(1, cols):
-        unit_copy(step).wait()
-    for q in range(nq):
-        for step in range(1, cols):
-            part_copy(step, q).wait()
-            coded = got[step - 1, q].astype(jnp.float32)
-            root = jnp.exp(0.125 * jnp.log(jnp.abs(coded)))
-            root = jnp.where(coded < 0.0, -root, jnp.where(coded > 0.0, root, 0.0))
-            before = own_ref[q] if step == 1 else total[...]
-            total[...] = before + root * got_unit[step - 1, q, 0:1, 0:1]
-        out_ref[q] = jnp.where(live, total[...], 0.0).astype(out_ref.dtype)
+    vertical = lax.broadcasted_iota(jnp.int32, (strip, 1), 0) + lax.rem(first_row, width)
+
+    total[...] = jnp.zeros(total.shape, jnp.float32)
+
+    @pl.loop(0, nq)
+    def finish(q):
+        for up, side in ((1, sides[0]), (0, sides[1])):
+            @pl.when(side)
+            def arrived():
+                copy(up, me, q).wait_recv()
+                unit = unit_of(up, me, q)
+                for at in range(0, rows_out, strip):
+                    if up:
+                        before = own(me, q, at)
+                    else:
+                        before = jnp.where(sides[0], total[pl.ds(at, strip), :], own(me, q, at))
+                    total[pl.ds(at, strip), :] = before + decode(up, me, q, at, unit)
+        for at in range(0, rows_out, strip):
+            kept = jnp.where(vertical + at < size, total[pl.ds(at, strip), :], 0.0)
+            out_ref[q, pl.ds(at, strip), :] = kept.astype(out_ref.dtype)
+
+    @pl.loop(0, cols * nq)
+    def drain(k):
+        @pl.when(me != k // nq)
+        def sent():
+            copy(1, k // nq, k % nq).wait_send()
 
 
 def on_device(screen, values, sizes, slot, orbitals):
@@ -247,39 +277,32 @@
     )(order, labels, values)
 
     rows_out = per_row * width // cols
-    packed, units, own = pl.pallas_call(
+    totals = pl.pallas_call(
         functools.partial(contract_kernel, capacity, per_col),
-        out_shape=[
-            jax.ShapeDtypeStruct((cols, NQ, rows_out, orbital_count), jnp.bfloat16),
-            jax.ShapeDtypeStruct((cols, NQ, 8, LANES), jnp.float32),
-            jax.ShapeDtypeStruct((NQ, rows_out, orbital_count), jnp.float32),
-        ],
+        out_shape=jax.ShapeDtypeStruct((per_row * NQ, width, orbital_count), jnp.float32),
         in_specs=[smem, smem, vmem, vmem],
-        out_specs=[vmem] * 3,
-        scratch_shapes=[
-            pltpu.VMEM((per_row * NQ, width, orbital_count), jnp.float32),
-            pltpu.VMEM((per_col, width, orbital_count), orbitals.dtype),
-        ],
+        out_specs=vmem,
+        scratch_shapes=[pltpu.VMEM((per_col, width, orbital_count), orbitals.dtype)],
         compiler_params=pltpu.CompilerParams(vmem_limit_bytes=VMEM_LIMIT),
         name="contract_blocks",
     )(got_labels, sizes, got, orbitals)
 
     summed = pl.pallas_call(
-        functools.partial(scatter_kernel, cols, blocks_all, width),
+        functools.partial(scatter_kernel, cols, blocks_all),
         out_shape=jax.ShapeDtypeStruct((NQ, rows_out, orbital_count), jnp.bfloat16),
-        in_specs=[smem, smem, vmem, vmem, vmem],
+        in_specs=[smem, smem, vmem],
         out_specs=vmem,
         scratch_shapes=[
-            pltpu.VMEM((cols - 1, NQ, rows_out, orbital_count), jnp.bfloat16),
-            pltpu.VMEM((cols - 1, NQ, 8, LANES), jnp.float32),
+            pltpu.VMEM((cols, NQ, rows_out + 16, orbital_count), jnp.bfloat16),
+            pltpu.VMEM((2, cols, NQ, rows_out + 16, orbital_count), jnp.bfloat16),
             pltpu.VMEM((rows_out, orbital_count), jnp.float32),
-            dma((cols - 1, NQ)), dma((cols - 1, NQ)), dma((cols - 1,)), dma((cols - 1,)),
+            dma((cols, NQ)), dma((2, cols, NQ)),
         ],
         compiler_params=pltpu.CompilerParams(
             collective_id=1, has_side_effects=True, vmem_limit_bytes=VMEM_LIMIT
         ),
         name="scatter_sums",
-    )(slot, sizes, packed, units, own)
+    )(slot, sizes, totals)
     return summed.transpose(1, 0, 2)
 
 

time: 95.5 us -> 84.4 us (0.88)
  Pallas kernels: 89.8 us -> 78.8 us
    pallas_call x1, Pallas kernels: 51 us -> 44.2 us  [on_device(): pl.pallas_call(functools.partial(scatter_kernel, cols, blocks_all), out_s...]
    pallas_call x1, Pallas kernels: 13.8 us -> 10.4 us  [on_device(): pl.pallas_call(functools.partial(contract_kernel, capacity, per_col), out...]
where the time goes in v2:
time: 84.4 us; the launch traced here: 84.2 us
  Pallas kernels  78.8 us (93%)
  local copies, waits for them, and re-layouts  5.26 us (6%)
    pallas_call x1, Pallas kernels, on_device(): pl.pallas_call(functools.partial(scatter_kernel, cols, blocks_all), out_s...  44.2 us
    pallas_call x1, Pallas kernels, on_device(): pl.pallas_call(functools.partial(exchange_kernel, rows, capacity), out_sh...  21.9 us
    pallas_call x1, Pallas kernels, on_device(): pl.pallas_call(functools.partial(contract_kernel, capacity, per_col), out...  10.4 us
    unnamed x13, local copies, waits for them, and re-layouts  4.06 us
    pallas_call x1, Pallas kernels, on_device(): pl.pallas_call(functools.partial(order_kernel, rows, capacity, per_row, p...  2.38 us

profile of v2, /device:TPU:9, one launch (start us, length us, event | category | flops | bytes accessed | tf_op | source)
XLA Modules:
  0.0 84.2 jit_solution(281943417489261898)
XLA Ops:
  0.0 0.0 copy-start.2
  0.0 1.4 %copy.6.screen_ref = s32[48,3]{1,0:T(8,128)} copy(s32[48,3]{0,1:T(4,128)} %param.5) | data formatting | bytes 1152 | tf_op args[0]
  1.4 2.4 %order_blocks.1 = (s32[48]{0:T(128)}, s32[48]{0:T(128)}) custom-call(s32[48,3]{1,0:T(8,128)} %copy.6.screen_ref, s32[32]{0:T(128)} %slot_ref.3), custom_call_target="tpu_custom_call" | custom-call | tf_op jit(solution)/shard_map/order_blocks/pallas_call | solution.py:251
  3.8 0.0 copy-start
  3.8 1.4 %copy-done = bf16[48,128,128]{2,1,0:T(8,128)(2,1)S(1)} copy-done((bf16[48,128,128]{2,1,0:T(8,128)(2,1)S(1)}, bf16[48,128,128]{2,1,0:T(8,128)(2,1)}, u32[]{:S(2)}) %copy-start) | copy-done | bytes 1572888
  5.2 0.0 copy-start.4
  5.2 0.6 copy-done.4
  5.8 0.0 copy-start.5
  5.8 0.7 copy-done.5
  6.4 0.0 copy-start.1
  6.4 21.9 %exchange_blocks.1 = (bf16[48,128,128]{2,1,0:T(8,128)(2,1)S(1)}, s32[8,1,128]{2,1,0:T(1,128)S(1)}) custom-call(s32[48]{0:T(128)S(1)} %copy-done.4, s32[48]{0:T(128)S(1)} %copy-done.5, bf16[48,128,128]{2,1,0:T(8,128)(2,1)S(1)} %copy-done), custom_call_target="tpu_custom_call" | custom-call | tf_op jit(solution)/shard_map/exchange_blocks/pallas_call | solution.py:260
  28.3 0.0 copy-done.2
  28.3 0.0 copy-done.1
  28.3 0.0 copy-start.3
  28.4 10.4 %contract_blocks.1.totals_ref = f32[16,128,512]{2,1,0:T(8,128)S(1)} custom-call(s32[8,1,128]{2,1,0:T(1,128)S(1)} %get-tuple-element.11.label_ref, s32[32]{0:T(128)S(1)} %copy-done.2, bf16[48,128,128]{2,1,0:T(8,128)(2,1)S(1)} %get-tuple-element.12.got_ref, bf16[1024,512]{1,0:T(8,128)(2,1)S(1)} %copy-done.1), custom_call_target="tpu_custom_call" | custom-call | tf_op jit(solution)/shard_map/contract_blocks/pallas_call | solution.py:280
  38.8 0.0 copy-done.3
  38.8 44.2 %scatter_sums.1 = bf16[4,128,512]{2,1,0:T(8,128)(2,1)S(1)} custom-call(s32[32]{0:T(128)S(1)} %copy-done.3, s32[32]{0:T(128)S(1)} %copy-done.2, f32[16,128,512]{2,1,0:T(8,128)S(1)} %contract_blocks.1.totals_ref), custom_call_target="tpu_custom_call" | custom-call | tf_op jit(solution)/shard_map/scatter_sums/pallas_call | solution.py:290
  83.0 1.2 %copy.7 = bf16[128,4,512]{2,1,0:T(4,128)(2,1)} copy(bf16[128,4,512]{2,0,1:T(8,128)(2,1)S(1)} %bitcast.1) | data formatting | bytes 1048576 | tf_op jit(solution)/shard_map/transpose | solution.py:306
Async XLA Ops:
  0.0 28.3 %copy-start.2 = (s32[32]{0:T(128)S(1)}, s32[32]{0:T(128)}, u32[]{:S(2)}) copy-start(s32[32]{0:T(128)} %sizes_ref.3) | copy-start | bytes 388
  3.8 1.4 %copy-start = (bf16[48,128,128]{2,1,0:T(8,128)(2,1)S(1)}, bf16[48,128,128]{2,1,0:T(8,128)(2,1)}, u32[]{:S(2)}) copy-start(bf16[48,128,128]{2,1,0:T(8,128)(2,1)} %values_ref.1) | copy-start | bytes 4718596
  5.2 0.6 copy-start.4
  5.8 0.7 copy-start.5
  6.4 21.9 %copy-start.1 = (bf16[1024,512]{1,0:T(8,128)(2,1)S(1)}, bf16[1024,512]{1,0:T(8,128)(2,1)}, u32[]{:S(2)}) copy-start(bf16[1024,512]{1,0:T(8,128)(2,1)} %orbitals_ref.1) | copy-start | bytes 3145732
  28.3 10.4 %copy-start.3 = (s32[32]{0:T(128)S(1)}, s32[32]{0:T(128)}, u32[]{:S(2)}) copy-start(s32[32]{0:T(128)} %slot_ref.3) | copy-start | bytes 388

commit v3 on v2

--- a/solution.py
+++ b/solution.py
@@ -107,19 +107,28 @@
     def clear(t):
         totals_ref[t] = jnp.zeros(totals_ref.shape[1:], jnp.float32)
 
-    @pl.loop(0, got_ref.shape[0], unroll=2)
-    def add(k):
-        label = label_ref[k // capacity, 0, k % capacity]
-
-        @pl.when(label >= 0)
-        def listed():
-            totals_ref[label // per_col] += jnp.dot(
-                got_ref[k], coeffs[label % per_col], preferred_element_type=jnp.float32
+    group = 4
+
+    @pl.loop(0, got_ref.shape[0] // group)
+    def add(g):
+        places = [g * group + j for j in range(group)]
+        labels = [label_ref[k // capacity, 0, k % capacity] for k in places]
+        products = [
+            jnp.dot(
+                got_ref[k], coeffs[jnp.maximum(label, 0) % per_col],
+                preferred_element_type=jnp.float32,
             )
+            for k, label in zip(places, labels)
+        ]
+        for label, product in zip(labels, products):
+            @pl.when(label >= 0)
+            def listed():
+                totals_ref[label // per_col] += product
 
 
 def scatter_kernel(
-    cols, blocks_all, slot_ref, sizes_ref, totals_ref, out_ref, send, got, total, send_sem, recv_sem
+    cols, blocks_all, slot_ref, sizes_ref, totals_ref, out_ref, send, got, send_unit, got_unit, total,
+    send_sem, recv_sem, send_unit_sem, recv_unit_sem,
 ):
     me = lax.axis_index("col")
     nq, rows_out, orbital_count = out_ref.shape
@@ -134,15 +143,41 @@
         )
     pl.semaphore_wait(barrier, cols - 1)
 
-    def copy(up, target, q):
-        return pltpu.make_async_remote_copy(
-            src_ref=send.at[target, q],
-            dst_ref=got.at[up, target, q],
-            send_sem=send_sem.at[target, q],
-            recv_sem=recv_sem.at[up, target, q],
-            device_id={"col": me + 1 if up else me - 1},
-            device_id_type=pl.DeviceIdType.MESH,
-        )
+    class Pair:
+        def __init__(self, up, target, q):
+            where = dict(
+                device_id={"col": me + 1 if up else me - 1}, device_id_type=pl.DeviceIdType.MESH
+            )
+            self.both = (
+                pltpu.make_async_remote_copy(
+                    src_ref=send_unit.at[target, q],
+                    dst_ref=got_unit.at[up, target, q],
+                    send_sem=send_unit_sem.at[target, q],
+                    recv_sem=recv_unit_sem.at[up, target, q],
+                    **where,
+                ),
+                pltpu.make_async_remote_copy(
+                    src_ref=send.at[target, q],
+                    dst_ref=got.at[up, target, q],
+                    send_sem=send_sem.at[target, q],
+                    recv_sem=recv_sem.at[up, target, q],
+                    **where,
+                ),
+            )
+
+        def start(self):
+            for each in self.both:
+                each.start()
+
+        def wait_recv(self):
+            for each in self.both:
+                each.wait_recv()
+
+        def wait_send(self):
+            for each in self.both:
+                each.wait_send()
+
+    copy = Pair
 
     strip = min(rows_out, 32)
 
@@ -156,7 +191,7 @@
         return jnp.where(coded < 0.0, -root, root) * unit
 
     def unit_of(up, c, q):
-        return got[up, c, q, pl.ds(rows_out, 16), :].astype(jnp.float32)[0:1, :]
+        return got_unit[up, c, q, 0:1, 0:1]
 
     def code(c, q, parts):
         top = jnp.zeros((8, orbital_count), jnp.float32)
@@ -165,9 +200,9 @@
             total[pl.ds(at, strip), :] = part
             top = jnp.maximum(top, jnp.max(jnp.abs(part).reshape(-1, 8, orbital_count), axis=0))
         top = jnp.max(jnp.max(top, axis=0, keepdims=True), axis=1, keepdims=True)
-        unit = (jnp.maximum(top, 1e-30) * (1.01 * 2.0**-15)).astype(send.dtype)
-        send[c, q, pl.ds(rows_out, 16), :] = jnp.broadcast_to(unit, (16, orbital_count))
-        inverse = 1.0 / unit.astype(jnp.float32)
+        unit = jnp.maximum(top, 1e-30) * 2.0**-15
+        send_unit[c, q] = jnp.broadcast_to(unit, (8, LANES))
+        inverse = 1.0 / unit
         for at in range(0, rows_out, strip):
             scaled = total[pl.ds(at, strip), :] * inverse
             power = scaled * scaled
@@ -293,10 +328,12 @@
         in_specs=[smem, smem, vmem],
         out_specs=vmem,
         scratch_shapes=[
-            pltpu.VMEM((cols, NQ, rows_out + 16, orbital_count), jnp.bfloat16),
-            pltpu.VMEM((2, cols, NQ, rows_out + 16, orbital_count), jnp.bfloat16),
+            pltpu.VMEM((cols, NQ, rows_out, orbital_count), jnp.bfloat16),
+            pltpu.VMEM((2, cols, NQ, rows_out, orbital_count), jnp.bfloat16),
+            pltpu.VMEM((cols, NQ, 8, LANES), jnp.float32),
+            pltpu.VMEM((2, cols, NQ, 8, LANES), jnp.float32),
             pltpu.VMEM((rows_out, orbital_count), jnp.float32),
-            dma((cols, NQ)), dma((2, cols, NQ)),
+            dma((cols, NQ)), dma((2, cols, NQ)), dma((cols, NQ)), dma((2, cols, NQ)),
         ],
         compiler_params=pltpu.CompilerParams(
             collective_id=1, has_side_effects=True, vmem_limit_bytes=VMEM_LIMIT

time: 84.4 us -> 77.5 us (0.918)
  Pallas kernels: 78.8 us -> 71.9 us
    pallas_call x1, Pallas kernels: 10.4 us -> 6.16 us  [on_device(): pl.pallas_call(functools.partial(contract_kernel, capacity, per_col), out...]
    pallas_call x1, Pallas kernels: 44.2 us -> 41.5 us  [on_device(): pl.pallas_call(functools.partial(scatter_kernel, cols, blocks_all), out_s...]
where the time goes in v3:
time: 77.5 us; the launch traced here: 77.2 us
  Pallas kernels  71.9 us (93%)
  local copies, waits for them, and re-layouts  5.26 us (7%)
    pallas_call x1, Pallas kernels, on_device(): pl.pallas_call(functools.partial(scatter_kernel, cols, blocks_all), out_s...  41.5 us
    pallas_call x1, Pallas kernels, on_device(): pl.pallas_call(functools.partial(exchange_kernel, rows, capacity), out_sh...  21.9 us
    pallas_call x1, Pallas kernels, on_device(): pl.pallas_call(functools.partial(contract_kernel, capacity, per_col), out...  6.16 us
    unnamed x13, local copies, waits for them, and re-layouts  4.06 us
    pallas_call x1, Pallas kernels, on_device(): pl.pallas_call(functools.partial(order_kernel, rows, capacity, per_row, p...  2.38 us

profile of v3, /device:TPU:9, one launch (start us, length us, event | category | flops | bytes accessed | tf_op | source)
XLA Modules:
  0.0 77.2 jit_solution(6967573774236051453)
XLA Ops:
  0.0 0.0 copy-start.2
  0.0 1.4 %copy.6.screen_ref = s32[48,3]{1,0:T(8,128)} copy(s32[48,3]{0,1:T(4,128)} %param.5) | data formatting | bytes 1152 | tf_op args[0]
  1.4 2.4 %order_blocks.1 = (s32[48]{0:T(128)}, s32[48]{0:T(128)}) custom-call(s32[48,3]{1,0:T(8,128)} %copy.6.screen_ref, s32[32]{0:T(128)} %slot_ref.3), custom_call_target="tpu_custom_call" | custom-call | tf_op jit(solution)/shard_map/order_blocks/pallas_call | solution.py:286
  3.8 0.0 copy-start
  3.8 1.4 %copy-done = bf16[48,128,128]{2,1,0:T(8,128)(2,1)S(1)} copy-done((bf16[48,128,128]{2,1,0:T(8,128)(2,1)S(1)}, bf16[48,128,128]{2,1,0:T(8,128)(2,1)}, u32[]{:S(2)}) %copy-start) | copy-done | bytes 1572888
  5.2 0.0 copy-start.4
  5.2 0.6 copy-done.4
  5.8 0.0 copy-start.5
  5.8 0.7 copy-done.5
  6.4 0.0 copy-start.1
  6.4 21.9 %exchange_blocks.1 = (bf16[48,128,128]{2,1,0:T(8,128)(2,1)S(1)}, s32[8,1,128]{2,1,0:T(1,128)S(1)}) custom-call(s32[48]{0:T(128)S(1)} %copy-done.4, s32[48]{0:T(128)S(1)} %copy-done.5, bf16[48,128,128]{2,1,0:T(8,128)(2,1)S(1)} %copy-done), custom_call_target="tpu_custom_call" | custom-call | tf_op jit(solution)/shard_map/exchange_blocks/pallas_call | solution.py:295
  28.3 0.0 copy-done.2
  28.3 0.0 copy-done.1
  28.3 0.0 copy-start.3
  28.4 6.2 %contract_blocks.1.totals_ref = f32[16,128,512]{2,1,0:T(8,128)S(1)} custom-call(s32[8,1,128]{2,1,0:T(1,128)S(1)} %get-tuple-element.11.label_ref, s32[32]{0:T(128)S(1)} %copy-done.2, bf16[48,128,128]{2,1,0:T(8,128)(2,1)S(1)} %get-tuple-element.12.got_ref, bf16[1024,512]{1,0:T(8,128)(2,1)S(1)} %copy-done.1), custom_call_target="tpu_custom_call" | custom-call | tf_op jit(solution)/shard_map/contract_blocks/pallas_call | solution.py:315
  34.5 0.0 copy-done.3
  34.5 41.5 %scatter_sums.1 = bf16[4,128,512]{2,1,0:T(8,128)(2,1)S(1)} custom-call(s32[32]{0:T(128)S(1)} %copy-done.3, s32[32]{0:T(128)S(1)} %copy-done.2, f32[16,128,512]{2,1,0:T(8,128)S(1)} %contract_blocks.1.totals_ref), custom_call_target="tpu_custom_call" | custom-call | tf_op jit(solution)/shard_map/scatter_sums/pallas_call | solution.py:325
  76.0 1.2 %copy.7 = bf16[128,4,512]{2,1,0:T(4,128)(2,1)} copy(bf16[128,4,512]{2,0,1:T(8,128)(2,1)S(1)} %bitcast.1) | data formatting | bytes 1048576 | tf_op jit(solution)/shard_map/transpose | solution.py:343
Async XLA Ops:
  0.0 28.3 %copy-start.2 = (s32[32]{0:T(128)S(1)}, s32[32]{0:T(128)}, u32[]{:S(2)}) copy-start(s32[32]{0:T(128)} %sizes_ref.3) | copy-start | bytes 388
  3.8 1.4 %copy-start = (bf16[48,128,128]{2,1,0:T(8,128)(2,1)S(1)}, bf16[48,128,128]{2,1,0:T(8,128)(2,1)}, u32[]{:S(2)}) copy-start(bf16[48,128,128]{2,1,0:T(8,128)(2,1)} %values_ref.1) | copy-start | bytes 4718596
  5.2 0.6 copy-start.4
  5.8 0.7 copy-start.5
  6.4 21.9 %copy-start.1 = (bf16[1024,512]{1,0:T(8,128)(2,1)S(1)}, bf16[1024,512]{1,0:T(8,128)(2,1)}, u32[]{:S(2)}) copy-start(bf16[1024,512]{1,0:T(8,128)(2,1)} %orbitals_ref.1) | copy-start | bytes 3145732
  28.3 6.2 %copy-start.3 = (s32[32]{0:T(128)S(1)}, s32[32]{0:T(128)}, u32[]{:S(2)}) copy-start(s32[32]{0:T(128)} %slot_ref.3) | copy-start | bytes 388

commit v4 on v3

--- a/solution.py
+++ b/solution.py
@@ -76,12 +76,13 @@
             ),
         )
 
-    pl.semaphore_wait(barrier, rows - 1)
     for step in range(1, rows):
         target = lax.rem(me + step, rows)
         for j in range(capacity):
             send[step - 1, j] = values_ref[order_ref[target * capacity + j]]
         send_label[step - 1] = fill_label(target)
+    pl.semaphore_wait(barrier, rows - 1)
+    for step in range(1, rows):
         for copy in copies(step):
             copy.start()
     for j in range(capacity):
@@ -107,7 +108,7 @@
     def clear(t):
         totals_ref[t] = jnp.zeros(totals_ref.shape[1:], jnp.float32)
 
-    group = 4
+    group = 8
 
     @pl.loop(0, got_ref.shape[0] // group)
     def add(g):

time: 77.5 us -> 76.6 us (0.988)
  Pallas kernels: 71.9 us -> 71 us
    pallas_call x1, Pallas kernels: 6.16 us -> 5.27 us  [on_device(): pl.pallas_call(functools.partial(contract_kernel, capacity, per_col), out...]
where the time goes in v4:
time: 76.6 us; the launch traced here: 76.4 us
  Pallas kernels  71 us (93%)
  local copies, waits for them, and re-layouts  5.26 us (7%)
    pallas_call x1, Pallas kernels, on_device(): pl.pallas_call(functools.partial(scatter_kernel, cols, blocks_all), out_s...  41.5 us
    pallas_call x1, Pallas kernels, on_device(): pl.pallas_call(functools.partial(exchange_kernel, rows, capacity), out_sh...  21.8 us
    pallas_call x1, Pallas kernels, on_device(): pl.pallas_call(functools.partial(contract_kernel, capacity, per_col), out...  5.27 us
    unnamed x13, local copies, waits for them, and re-layouts  4.06 us
    pallas_call x1, Pallas kernels, on_device(): pl.pallas_call(functools.partial(order_kernel, rows, capacity, per_row, p...  2.38 us

profile of v4, /device:TPU:9, one launch (start us, length us, event | category | flops | bytes accessed | tf_op | source)
XLA Modules:
  0.0 76.4 jit_solution(11571440503796362874)
XLA Ops:
  0.0 0.0 copy-start.2
  0.0 1.4 %copy.6.screen_ref = s32[48,3]{1,0:T(8,128)} copy(s32[48,3]{0,1:T(4,128)} %param.5) | data formatting | bytes 1152 | tf_op args[0]
  1.4 2.4 %order_blocks.1 = (s32[48]{0:T(128)}, s32[48]{0:T(128)}) custom-call(s32[48,3]{1,0:T(8,128)} %copy.6.screen_ref, s32[32]{0:T(128)} %slot_ref.3), custom_call_target="tpu_custom_call" | custom-call | tf_op jit(solution)/shard_map/order_blocks/pallas_call | solution.py:287
  3.8 0.0 copy-start
  3.8 1.4 %copy-done = bf16[48,128,128]{2,1,0:T(8,128)(2,1)S(1)} copy-done((bf16[48,128,128]{2,1,0:T(8,128)(2,1)S(1)}, bf16[48,128,128]{2,1,0:T(8,128)(2,1)}, u32[]{:S(2)}) %copy-start) | copy-done | bytes 1572888
  5.2 0.0 copy-start.4
  5.2 0.6 copy-done.4
  5.8 0.0 copy-start.5
  5.8 0.7 copy-done.5
  6.4 0.0 copy-start.1
  6.4 21.8 %exchange_blocks.1 = (bf16[48,128,128]{2,1,0:T(8,128)(2,1)S(1)}, s32[8,1,128]{2,1,0:T(1,128)S(1)}) custom-call(s32[48]{0:T(128)S(1)} %copy-done.4, s32[48]{0:T(128)S(1)} %copy-done.5, bf16[48,128,128]{2,1,0:T(8,128)(2,1)S(1)} %copy-done), custom_call_target="tpu_custom_call" | custom-call | tf_op jit(solution)/shard_map/exchange_blocks/pallas_call | solution.py:296
  28.3 0.0 copy-done.2
  28.3 0.0 copy-done.1
  28.3 0.0 copy-start.3
  28.3 5.3 %contract_blocks.1.totals_ref = f32[16,128,512]{2,1,0:T(8,128)S(1)} custom-call(s32[8,1,128]{2,1,0:T(1,128)S(1)} %get-tuple-element.11.label_ref, s32[32]{0:T(128)S(1)} %copy-done.2, bf16[48,128,128]{2,1,0:T(8,128)(2,1)S(1)} %get-tuple-element.12.got_ref, bf16[1024,512]{1,0:T(8,128)(2,1)S(1)} %copy-done.1), custom_call_target="tpu_custom_call" | custom-call | tf_op jit(solution)/shard_map/contract_blocks/pallas_call | solution.py:316
  33.6 0.0 copy-done.3
  33.6 41.5 %scatter_sums.1 = bf16[4,128,512]{2,1,0:T(8,128)(2,1)S(1)} custom-call(s32[32]{0:T(128)S(1)} %copy-done.3, s32[32]{0:T(128)S(1)} %copy-done.2, f32[16,128,512]{2,1,0:T(8,128)S(1)} %contract_blocks.1.totals_ref), custom_call_target="tpu_custom_call" | custom-call | tf_op jit(solution)/shard_map/scatter_sums/pallas_call | solution.py:326
  75.2 1.2 %copy.7 = bf16[128,4,512]{2,1,0:T(4,128)(2,1)} copy(bf16[128,4,512]{2,0,1:T(8,128)(2,1)S(1)} %bitcast.1) | data formatting | bytes 1048576 | tf_op jit(solution)/shard_map/transpose | solution.py:344
Async XLA Ops:
  0.0 28.3 %copy-start.2 = (s32[32]{0:T(128)S(1)}, s32[32]{0:T(128)}, u32[]{:S(2)}) copy-start(s32[32]{0:T(128)} %sizes_ref.3) | copy-start | bytes 388
  3.8 1.4 %copy-start = (bf16[48,128,128]{2,1,0:T(8,128)(2,1)S(1)}, bf16[48,128,128]{2,1,0:T(8,128)(2,1)}, u32[]{:S(2)}) copy-start(bf16[48,128,128]{2,1,0:T(8,128)(2,1)} %values_ref.1) | copy-start | bytes 4718596
  5.2 0.6 copy-start.4
  5.8 0.7 copy-start.5
  6.4 21.9 %copy-start.1 = (bf16[1024,512]{1,0:T(8,128)(2,1)S(1)}, bf16[1024,512]{1,0:T(8,128)(2,1)}, u32[]{:S(2)}) copy-start(bf16[1024,512]{1,0:T(8,128)(2,1)} %orbitals_ref.1) | copy-start | bytes 3145732
  28.3 5.3 %copy-start.3 = (s32[32]{0:T(128)S(1)}, s32[32]{0:T(128)}, u32[]{:S(2)}) copy-start(s32[32]{0:T(128)} %slot_ref.3) | copy-start | bytes 388
